TPU v7x, 32 devices: a whole 2x2x4 slice. The times are simulated.
32 devices in a mesh: rep: 2 (over x), led: 16 (over z, y, core).
Axes of the slice: x: 2, y: 2, z: 4, core: 2. Of those that a mesh axis runs over, the one named last changes fastest.
Arguments:
- spectrum: bfloat16 [96, 16, 2, 6144], P(('rep', 'led')), parts along dimension 0, may hold values from -6 to 6
- block_owner: int32 [24], replicated, may hold values from 0 to 15, as said below
- row_offset: int32 [16], replicated, may hold values from 0 to 128
- column_offset: int32 [16], replicated, may hold values from 0 to 5888
- pupil_modes: bfloat16 [8, 2, 256, 256], replicated, may hold values from -6 to 6
- amplitude: float32 [32, 512, 512], P(('rep', 'led')), parts along dimension 0, may hold values from 1 to 4
Outputs:
- spectrum_grad: float32 [96, 16, 2, 6144], P(('rep', 'led')), parts along dimension 0
There are 2 independent parts, one for each index of `rep`. A program takes and returns all parts, laid end to end along the dimension named above; an argument that names none is the same for every part. Nothing has to cross between parts.
Inputs may be any that keep to these rules, and one draw needn't show every extreme that they name: `block_owner`: every device owns 1 to 3 blocks and some device owns exactly 3; a device's blocks fill its first slots in increasing block order, and no output reads its remaining slots.
All inputs are finite; a program needn't handle non-finite values.
Results may differ from a plain program's by a relative error of at most 0.0095.
Values may be sent and summed in bfloat16 or wider, within the bound.
A program may use at most 128 MiB of HBM per device.

v0:
```python
import math

import jax
import jax.numpy as jnp
from jax import lax
from jax.sharding import PartitionSpec as P

amp_eps = 0.1


def slot_map(block_owner, slot_count):
    order = jnp.arange(block_owner.shape[0], dtype=jnp.int32)
    same_before = (block_owner[None, :] == block_owner[:, None]) & (order[None, :] < order[:, None])
    rank_in_owner = jnp.sum(same_before.astype(jnp.int32), axis=1)
    return block_owner * slot_count + rank_in_owner


def dft_tables(image_side, window_side):
    pixel = jnp.arange(image_side, dtype=jnp.int32)[:, None]
    freq = jnp.arange(window_side, dtype=jnp.int32)[None, :] - window_side // 2
    phase = jnp.mod(pixel * freq, image_side).astype(jnp.float32) * (2.0 * math.pi / image_side)
    scale = 1.0 / math.sqrt(image_side)
    real_part = (jnp.cos(phase) * scale).astype(jnp.bfloat16)
    imag_part = (jnp.sin(phase) * scale).astype(jnp.bfloat16)
    left_table = jnp.stack([jnp.stack([real_part, -imag_part]), jnp.stack([imag_part, real_part])])
    right_table = jnp.stack(
        [jnp.stack([real_part.T, imag_part.T]), jnp.stack([-imag_part.T, real_part.T])]
    )
    return (left_table, right_table)


def mode_gradient(window, pupil_modes, image_amp, left_table, right_table):
    spec_real = window[0].astype(jnp.float32)
    spec_imag = window[1].astype(jnp.float32)
    pupil_real = pupil_modes[:, 0].astype(jnp.float32)
    pupil_imag = pupil_modes[:, 1].astype(jnp.float32)
    pupil_field = jnp.stack(
        [
            spec_real * pupil_real - spec_imag * pupil_imag,
            spec_real * pupil_imag + spec_imag * pupil_real,
        ],
        axis=1,
    ).astype(jnp.bfloat16)
    half_transform = jnp.einsum(
        "kcuv,cdvq->kduq", pupil_field, right_table, preferred_element_type=jnp.float32
    ).astype(jnp.bfloat16)
    image_field = jnp.einsum(
        "edpu,kduq->kepq", left_table, half_transform, preferred_element_type=jnp.float32
    )
    intensity = jnp.sum(image_field * image_field, axis=(0, 1))
    modulus = jnp.sqrt(intensity + amp_eps)
    weight = (modulus - image_amp) / modulus
    field_grad = (image_field * weight[None, None]).astype(jnp.bfloat16)
    back_half = jnp.einsum(
        "deup,kepq->kduq", right_table, field_grad, preferred_element_type=jnp.float32
    ).astype(jnp.bfloat16)
    window_grad = jnp.einsum(
        "kduq,dcqv->kcuv", back_half, left_table, preferred_element_type=jnp.float32
    )
    grad_real = jnp.sum(pupil_real * window_grad[:, 0] + pupil_imag * window_grad[:, 1], axis=0)
    grad_imag = jnp.sum(pupil_real * window_grad[:, 1] - pupil_imag * window_grad[:, 0], axis=0)
    return jnp.stack([grad_real, grad_imag])


def shards(spectrum, block_owner, row_offset, column_offset, pupil_modes, amplitude):
    slot_count, block_rows, _, columns = spectrum.shape
    led_count = lax.axis_size("led")
    device = lax.axis_index("led")
    window_side = pupil_modes.shape[2]
    image_side = amplitude.shape[1]
    block_count = block_owner.shape[0]
    total_slots = led_count * slot_count
    slot_of_block = slot_map(block_owner, slot_count)
    matches = slot_of_block[None, :] == jnp.arange(total_slots, dtype=jnp.int32)[:, None]
    block_of_slot = jnp.sum(
        jnp.where(matches, jnp.arange(block_count, dtype=jnp.int32)[None, :], 0), axis=1
    )
    filled = jnp.any(matches, axis=1)
    row_ids = jnp.where(
        filled[:, None],
        block_of_slot[:, None] * block_rows + jnp.arange(block_rows, dtype=jnp.int32)[None, :],
        -1,
    ).reshape(-1)
    my_row = row_offset[device]
    my_column = column_offset[device]
    chosen_rows = row_ids[None, :] == my_row + jnp.arange(window_side, dtype=jnp.int32)[:, None]
    select_half = chosen_rows.astype(jnp.bfloat16)
    select_full = chosen_rows.astype(jnp.float32)
    left_table, right_table = dft_tables(image_side, window_side)
    shard_piece = lax.all_gather(spectrum, "led", axis=0, tiled=True)
    piece_slots = shard_piece.shape[0]
    cropped = lax.dynamic_slice_in_dim(shard_piece, my_column, window_side, 3)
    cropped = cropped.reshape(piece_slots * block_rows, 2, window_side)
    window = jnp.einsum(
        "wj,jcv->cwv", select_half, cropped, preferred_element_type=jnp.float32
    ).astype(jnp.bfloat16)
    gradient = mode_gradient(window, pupil_modes, amplitude[0], left_table, right_table)
    strips_back = jnp.einsum("wj,cwv->jcv", select_full, gradient, precision=lax.Precision.HIGHEST)
    strips_back = strips_back.reshape(led_count, slot_count, block_rows, 2, window_side)
    returned = lax.all_to_all(strips_back, "led", split_axis=0, concat_axis=0, tiled=True)

    def add_strip(led_index, running):
        start = column_offset[led_index]
        strip = lax.dynamic_index_in_dim(returned, led_index, 0, keepdims=False)
        current = lax.dynamic_slice_in_dim(running, start, window_side, 3)
        return lax.dynamic_update_slice_in_dim(running, current + strip, start, 3)

    result = jnp.zeros((slot_count, block_rows, 2, columns), jnp.float32)
    return lax.fori_loop(0, led_count, add_strip, result)


def solution(mesh):
    return jax.shard_map(
        shards,
        mesh=mesh,
        in_specs=(
            P(("rep", "led"), None, None, None),
            P(),
            P(),
            P(),
            P(),
            P(("rep", "led"), None, None),
        ),
        out_specs=P(("rep", "led"), None, None, None),
        check_vma=False,
    )
```

profile of v0, /device:TPU:1, one launch (start us, length us, event | category | flops | bytes accessed | tf_op | source)
XLA Modules:
  0.0 386.7 jit_solution(8084744443797909271)
XLA Ops:
  6.6 2.7 copy.39
  24.5 86.4 %all-gather.2.cloned.1.call-done = bf16[48,16,2,6144]{3,1,0,2:T(8,128)(2,1)} async-done(((bf16[3,16,2,6144]{3,1,0,2:T(8,128)(2,1)}), bf16[48,16,2,6144]{3,1,0,2:T(8,128)(2,1)}) %all-gather.2.cloned.1.call-update) | async-done | bytes 18874384 | tf_op jit(solution)/shard_map/all_gather | solution.py:90
  120.9 8.2 %fusion = (f32[512,512]{0,1:T(8,128)S(1)}, f32[8,512,2,512,1]{3,1,4,2,0:T(8,128)}) fusion(bf16[1,2,512,256]{3,2,1,0:T(8,128)(2,1)S(1)} %copy-done.6, bf16[1,2,512,256]{3,2,1,0:T(8,128)(2,1)S(1)} %copy-done.5, bf16[2,512,8,256,1]{3,1,4,0,2:T(8,128)(2,1)S(1)} %fusion.27), kind=kOutput, calls=%fused_computation.3 | convolution fusion | flops 4305190912 | bytes 23068672 | tf_op jit(solution)/shard_map/edpu,kduq->kepq/dot_general | solution.py:47
  130.4 12.4 %fusion.12 = f32[8,2,256,256]{3,2,1,0:T(8,128)} fusion(f32[8,512,2,512,1]{3,1,4,2,0:T(8,128)} %get-tuple-element.108, f32[512,512]{0,1:T(8,128)} %subtract_divide_fusion, bf16[1,2,256,512]{2,3,0,1:T(8,128)(2,1)} %get-tuple-element.100, bf16[1,2,256,512]{2,3,0,1:T(8,128)(2,1)} %get-tuple-element.99, bf16[1,2,512,256]{3,2,1,0:T(8,128)(2,1)} %get-tuple-element.98, ...), kind=kOutput, calls=%fused_computation.22 | convolution fusion | flops 6457131008 | bytes 24117248 | tf_op jit(solution)/shard_map/kduq,dcqv->kcuv/dot_general | solution.py:57
  142.8 3.0 fusion.24
  149.2 4.9 %all-to-all-start = ((f32[16,3,16,2,256]{4,3,2,1,0:T(2,128)}), f32[16,3,16,2,256]{4,3,2,1,0:T(2,128)}, u32[]{:S(2)}, u32[]{:S(2)}) async-start(f32[16,3,16,2,256]{4,3,2,1,0:T(2,128)} %copy.53), calls=%async_computation | async-start | bytes 3145728 | tf_op jit(solution)/shard_map/all_to_all | solution.py:100
  154.0 32.4 %all-to-all-done = f32[16,3,16,2,256]{4,3,2,1,0:T(2,128)} async-done(((f32[16,3,16,2,256]{4,3,2,1,0:T(2,128)}), f32[16,3,16,2,256]{4,3,2,1,0:T(2,128)}, u32[]{:S(2)}, u32[]{:S(2)}) %all-to-all-start) | async-done | bytes 1572896 | tf_op jit(solution)/shard_map/all_to_all | solution.py:100
  187.6 190.9 %while.13 = (s32[]{:T(128)}, f32[3,16,2,6144]{3,2,1,0:T(2,128)S(1)}, s32[16]{0:T(128)S(1)}, f32[16,3,16,2,256]{4,3,2,1,0:T(2,128)}, s32[]{:T(128)}, /*index=5*/s32[]{:T(128)}, s32[]{:T(128)}) while((s32[]{:T(128)}, f32[3,16,2,6144]{3,2,1,0:T(2,128)S(1)}, s32[16]{0:T(128)S(1)}, f32[16,3,16,2,256]{4,3,2,1,0:T(2,128)}, s32[]{:T(128)}, ...), condition=%wide.region_7.8_spmd, body=%wide.region_6.7_spmd.sunk | while | flops 24581 | bytes 491655 | solution.py:109
  191.2 9.1 %dynamic_update_slice.8 = f32[3,16,2,6144]{3,2,1,0:T(2,128)S(1)} dynamic-update-slice(f32[3,16,2,6144]{3,2,1,0:T(2,128)S(1)} %get-tuple-element.142, f32[3,16,2,256]{3,2,1,0:T(2,128)S(1)} %bitcast_add_fusion.2, s32[]{:T(128)} %constant.63.clone.1..sunk, s32[]{:T(128)} %constant.63.clone.1..sunk, s32[]{:T(128)} %constant.63.clone.1..sunk, s32[]{:T(128)S(6)} %select_n.122) | dynamic-update-slice | bytes 196612 | tf_op jit(solution)/shard_map/while/body/eval_jaxpr/dynamic_update_slice | solution.py:106
  203.9 9.1 %dynamic_update_slice.8 = f32[3,16,2,6144]{3,2,1,0:T(2,128)S(1)} dynamic-update-slice(f32[3,16,2,6144]{3,2,1,0:T(2,128)S(1)} %get-tuple-element.142, f32[3,16,2,256]{3,2,1,0:T(2,128)S(1)} %bitcast_add_fusion.2, s32[]{:T(128)} %constant.63.clone.1..sunk, s32[]{:T(128)} %constant.63.clone.1..sunk, s32[]{:T(128)} %constant.63.clone.1..sunk, s32[]{:T(128)S(6)} %select_n.122) | dynamic-update-slice | bytes 196612 | tf_op jit(solution)/shard_map/while/body/eval_jaxpr/dynamic_update_slice | solution.py:106
  216.7 9.1 %dynamic_update_slice.8 = f32[3,16,2,6144]{3,2,1,0:T(2,128)S(1)} dynamic-update-slice(f32[3,16,2,6144]{3,2,1,0:T(2,128)S(1)} %get-tuple-element.142, f32[3,16,2,256]{3,2,1,0:T(2,128)S(1)} %bitcast_add_fusion.2, s32[]{:T(128)} %constant.63.clone.1..sunk, s32[]{:T(128)} %constant.63.clone.1..sunk, s32[]{:T(128)} %constant.63.clone.1..sunk, s32[]{:T(128)S(6)} %select_n.122) | dynamic-update-slice | bytes 196612 | tf_op jit(solution)/shard_map/while/body/eval_jaxpr/dynamic_update_slice | solution.py:106
  229.4 9.1 %dynamic_update_slice.8 = f32[3,16,2,6144]{3,2,1,0:T(2,128)S(1)} dynamic-update-slice(f32[3,16,2,6144]{3,2,1,0:T(2,128)S(1)} %get-tuple-element.142, f32[3,16,2,256]{3,2,1,0:T(2,128)S(1)} %bitcast_add_fusion.2, s32[]{:T(128)} %constant.63.clone.1..sunk, s32[]{:T(128)} %constant.63.clone.1..sunk, s32[]{:T(128)} %constant.63.clone.1..sunk, s32[]{:T(128)S(6)} %select_n.122) | dynamic-update-slice | bytes 196612 | tf_op jit(solution)/shard_map/while/body/eval_jaxpr/dynamic_update_slice | solution.py:106
  242.1 9.1 %dynamic_update_slice.8 = f32[3,16,2,6144]{3,2,1,0:T(2,128)S(1)} dynamic-update-slice(f32[3,16,2,6144]{3,2,1,0:T(2,128)S(1)} %get-tuple-element.142, f32[3,16,2,256]{3,2,1,0:T(2,128)S(1)} %bitcast_add_fusion.2, s32[]{:T(128)} %constant.63.clone.1..sunk, s32[]{:T(128)} %constant.63.clone.1..sunk, s32[]{:T(128)} %constant.63.clone.1..sunk, s32[]{:T(128)S(6)} %select_n.122) | dynamic-update-slice | bytes 196612 | tf_op jit(solution)/shard_map/while/body/eval_jaxpr/dynamic_update_slice | solution.py:106
  254.9 9.1 %dynamic_update_slice.8 = f32[3,16,2,6144]{3,2,1,0:T(2,128)S(1)} dynamic-update-slice(f32[3,16,2,6144]{3,2,1,0:T(2,128)S(1)} %get-tuple-element.142, f32[3,16,2,256]{3,2,1,0:T(2,128)S(1)} %bitcast_add_fusion.2, s32[]{:T(128)} %constant.63.clone.1..sunk, s32[]{:T(128)} %constant.63.clone.1..sunk, s32[]{:T(128)} %constant.63.clone.1..sunk, s32[]{:T(128)S(6)} %select_n.122) | dynamic-update-slice | bytes 196612 | tf_op jit(solution)/shard_map/while/body/eval_jaxpr/dynamic_update_slice | solution.py:106
  267.6 9.1 %dynamic_update_slice.8 = f32[3,16,2,6144]{3,2,1,0:T(2,128)S(1)} dynamic-update-slice(f32[3,16,2,6144]{3,2,1,0:T(2,128)S(1)} %get-tuple-element.142, f32[3,16,2,256]{3,2,1,0:T(2,128)S(1)} %bitcast_add_fusion.2, s32[]{:T(128)} %constant.63.clone.1..sunk, s32[]{:T(128)} %constant.63.clone.1..sunk, s32[]{:T(128)} %constant.63.clone.1..sunk, s32[]{:T(128)S(6)} %select_n.122) | dynamic-update-slice | bytes 196612 | tf_op jit(solution)/shard_map/while/body/eval_jaxpr/dynamic_update_slice | solution.py:106
  280.3 9.1 %dynamic_update_slice.8 = f32[3,16,2,6144]{3,2,1,0:T(2,128)S(1)} dynamic-update-slice(f32[3,16,2,6144]{3,2,1,0:T(2,128)S(1)} %get-tuple-element.142, f32[3,16,2,256]{3,2,1,0:T(2,128)S(1)} %bitcast_add_fusion.2, s32[]{:T(128)} %constant.63.clone.1..sunk, s32[]{:T(128)} %constant.63.clone.1..sunk, s32[]{:T(128)} %constant.63.clone.1..sunk, s32[]{:T(128)S(6)} %select_n.122) | dynamic-update-slice | bytes 196612 | tf_op jit(solution)/shard_map/while/body/eval_jaxpr/dynamic_update_slice | solution.py:106
  293.1 9.1 %dynamic_update_slice.8 = f32[3,16,2,6144]{3,2,1,0:T(2,128)S(1)} dynamic-update-slice(f32[3,16,2,6144]{3,2,1,0:T(2,128)S(1)} %get-tuple-element.142, f32[3,16,2,256]{3,2,1,0:T(2,128)S(1)} %bitcast_add_fusion.2, s32[]{:T(128)} %constant.63.clone.1..sunk, s32[]{:T(128)} %constant.63.clone.1..sunk, s32[]{:T(128)} %constant.63.clone.1..sunk, s32[]{:T(128)S(6)} %select_n.122) | dynamic-update-slice | bytes 196612 | tf_op jit(solution)/shard_map/while/body/eval_jaxpr/dynamic_update_slice | solution.py:106
  305.8 9.1 %dynamic_update_slice.8 = f32[3,16,2,6144]{3,2,1,0:T(2,128)S(1)} dynamic-update-slice(f32[3,16,2,6144]{3,2,1,0:T(2,128)S(1)} %get-tuple-element.142, f32[3,16,2,256]{3,2,1,0:T(2,128)S(1)} %bitcast_add_fusion.2, s32[]{:T(128)} %constant.63.clone.1..sunk, s32[]{:T(128)} %constant.63.clone.1..sunk, s32[]{:T(128)} %constant.63.clone.1..sunk, s32[]{:T(128)S(6)} %select_n.122) | dynamic-update-slice | bytes 196612 | tf_op jit(solution)/shard_map/while/body/eval_jaxpr/dynamic_update_slice | solution.py:106
  318.5 9.1 %dynamic_update_slice.8 = f32[3,16,2,6144]{3,2,1,0:T(2,128)S(1)} dynamic-update-slice(f32[3,16,2,6144]{3,2,1,0:T(2,128)S(1)} %get-tuple-element.142, f32[3,16,2,256]{3,2,1,0:T(2,128)S(1)} %bitcast_add_fusion.2, s32[]{:T(128)} %constant.63.clone.1..sunk, s32[]{:T(128)} %constant.63.clone.1..sunk, s32[]{:T(128)} %constant.63.clone.1..sunk, s32[]{:T(128)S(6)} %select_n.122) | dynamic-update-slice | bytes 196612 | tf_op jit(solution)/shard_map/while/body/eval_jaxpr/dynamic_update_slice | solution.py:106
  331.2 9.1 %dynamic_update_slice.8 = f32[3,16,2,6144]{3,2,1,0:T(2,128)S(1)} dynamic-update-slice(f32[3,16,2,6144]{3,2,1,0:T(2,128)S(1)} %get-tuple-element.142, f32[3,16,2,256]{3,2,1,0:T(2,128)S(1)} %bitcast_add_fusion.2, s32[]{:T(128)} %constant.63.clone.1..sunk, s32[]{:T(128)} %constant.63.clone.1..sunk, s32[]{:T(128)} %constant.63.clone.1..sunk, s32[]{:T(128)S(6)} %select_n.122) | dynamic-update-slice | bytes 196612 | tf_op jit(solution)/shard_map/while/body/eval_jaxpr/dynamic_update_slice | solution.py:106
  344.0 9.1 %dynamic_update_slice.8 = f32[3,16,2,6144]{3,2,1,0:T(2,128)S(1)} dynamic-update-slice(f32[3,16,2,6144]{3,2,1,0:T(2,128)S(1)} %get-tuple-element.142, f32[3,16,2,256]{3,2,1,0:T(2,128)S(1)} %bitcast_add_fusion.2, s32[]{:T(128)} %constant.63.clone.1..sunk, s32[]{:T(128)} %constant.63.clone.1..sunk, s32[]{:T(128)} %constant.63.clone.1..sunk, s32[]{:T(128)S(6)} %select_n.122) | dynamic-update-slice | bytes 196612 | tf_op jit(solution)/shard_map/while/body/eval_jaxpr/dynamic_update_slice | solution.py:106
  356.7 2.8 dynamic_update_slice.8
  363.1 2.6 dynamic_update_slice.8
  369.4 9.1 %dynamic_update_slice.8 = f32[3,16,2,6144]{3,2,1,0:T(2,128)S(1)} dynamic-update-slice(f32[3,16,2,6144]{3,2,1,0:T(2,128)S(1)} %get-tuple-element.142, f32[3,16,2,256]{3,2,1,0:T(2,128)S(1)} %bitcast_add_fusion.2, s32[]{:T(128)} %constant.63.clone.1..sunk, s32[]{:T(128)} %constant.63.clone.1..sunk, s32[]{:T(128)} %constant.63.clone.1..sunk, s32[]{:T(128)S(6)} %select_n.122) | dynamic-update-slice | bytes 196612 | tf_op jit(solution)/shard_map/while/body/eval_jaxpr/dynamic_update_slice | solution.py:106
  (83 shorter events, 57.1 us)
Async XLA Ops:
  6.5 2.8 copy-start.9
  6.5 4.5 %copy-start.7 = (s32[16]{0:T(128)S(1)}, s32[16]{0:T(128)}, u32[]{:S(2)}) copy-start(s32[16]{0:T(128)} %param.10) | copy-start | bytes 196
  6.5 5.1 %copy-start.8 = (s32[24]{0:T(128)S(1)}, s32[24]{0:T(128)}, u32[]{:S(2)}) copy-start(s32[24]{0:T(128)} %param.9) | copy-start | bytes 292
  6.5 5.7 %copy-start.2 = (f32[1,512,512]{2,1,0:T(8,128)S(1)}, f32[1,512,512]{2,1,0:T(8,128)}, u32[]{:S(2)}) copy-start(f32[1,512,512]{2,1,0:T(8,128)} %param.13) | copy-start | bytes 3145732
  6.5 104.4 %all-gather.2.cloned.1.call-start = ((), (), s32[]{:S(2)}) async-start(), calls=%async_computation.1 | async-start | bytes 20054016 | tf_op jit(solution)/shard_map/all_gather | solution.py:90
  112.6 4.3 %copy-start = (bf16[8,2,256,256]{3,2,1,0:T(8,128)(2,1)S(1)}, bf16[8,2,256,256]{3,2,1,0:T(8,128)(2,1)}, u32[]{:S(2)}) copy-start(bf16[8,2,256,256]{3,2,1,0:T(8,128)(2,1)} %param.12) | copy-start | bytes 6291460
  116.8 1.7 copy-start.3
  116.8 1.7 copy-start.4
  118.5 2.4 copy-start.5
  118.5 2.4 copy-start.6
  149.2 37.3 %all-to-all-start = ((f32[16,3,16,2,256]{4,3,2,1,0:T(2,128)}), f32[16,3,16,2,256]{4,3,2,1,0:T(2,128)}, u32[]{:S(2)}, u32[]{:S(2)}) async-start(f32[16,3,16,2,256]{4,3,2,1,0:T(2,128)} %copy.53), calls=%async_computation | async-start | bytes 3145728 | tf_op jit(solution)/shard_map/all_to_all | solution.py:100
  378.5 1.4 copy-start.1
Sparse Core Ops, SparseCore 0:
  9.4 101.4 all-gather.1
where the time goes:
time: 388 us; the launch traced here: 387 us
  local copies, waits for them, and re-layouts  156 us (40%)
  waiting for transfers between devices  119 us (31%)
  other arithmetic  35.8 us (9%)
  loops' own time  31.6 us (8%)
  matrix products  24.3 us (6%)
  between operations  15.3 us (4%)
  starting transfers between devices  4.89 us (1%)
    dynamic_update_slice x16, local copies, waits for them, and re-layouts, add_strip(): return lax.dynamic_update_slice_in_dim(running, current + strip, start, 3)  133 us
    all_gather x1, waiting for transfers between devices, shards(): shard_piece = lax.all_gather(spectrum, 'led', axis=0, tiled=True)  86.4 us
    all_to_all x1, waiting for transfers between devices, shards(): lax.all_to_all(strips_back, 'led', split_axis=0, concat_axis=0, tiled=True)  32.4 us
    another operation x1, loops' own time, shards(): return lax.fori_loop(0, led_count, add_strip, result)  31.6 us
    add x16, other arithmetic, add_strip(): return lax.dynamic_update_slice_in_dim(running, current + strip, start, 3)  17.1 us
    dot_general x1, matrix products, mode_gradient(): jnp.einsum('kduq,dcqv->kcuv', back_half, left_table, preferred_element_ty...  12.4 us
    dynamic_slice x16, local copies, waits for them, and re-layouts, add_strip(): start = column_offset[led_index]  9.38 us
    dot_general x1, matrix products, mode_gradient(): jnp.einsum('edpu,kduq->kepq', left_table, half_transform, preferred_eleme...  8.16 us
  transfers between devices with their start and end apart: 2, of which 2 were waited for; matrix products, arithmetic and copies ran while one was open for 3% of the time, Pallas kernels for 0%

commit v1 on v0

v1 whole, which is shorter than its diff:
```python
import functools
import math

import jax
import jax.numpy as jnp
import ml_dtypes
import numpy as np
from jax import lax
from jax.experimental import pallas as pl
from jax.experimental.pallas import tpu as pltpu
from jax.sharding import PartitionSpec as P

amp_eps = 0.1
f32 = jnp.float32
bf16 = jnp.bfloat16
VMEM = pl.BlockSpec(memory_space=pltpu.VMEM)
SMEM = pl.BlockSpec(memory_space=pltpu.SMEM)


def dft_tables(image_side, window_side):
    half = image_side // 2
    pixel = np.arange(half, dtype=np.int64)[:, None]
    freq = np.arange(window_side, dtype=np.int64)[None, :] - window_side // 2
    phase = np.mod(pixel * freq, image_side).astype(np.float64) * (2.0 * math.pi / image_side)
    scale = 1.0 / math.sqrt(image_side)
    real = (np.cos(phase) * scale).astype(np.float32).astype(ml_dtypes.bfloat16)
    imag = (np.sin(phase) * scale).astype(np.float32).astype(ml_dtypes.bfloat16)
    left = []
    for parity in (0, 1):
        a, b = real[:, parity::2], imag[:, parity::2]
        left.append(np.block([[a, -b], [b, a]]))
    left = np.stack(left)
    right = np.ascontiguousarray(left.transpose(0, 2, 1))
    return left, right


def deinterleave(side):
    order = np.concatenate([np.arange(0, side, 2), np.arange(1, side, 2)])
    perm = (np.arange(side)[:, None] == order[None, :]).astype(ml_dtypes.bfloat16)
    return perm, np.ascontiguousarray(perm.T)


def dot(a, b):
    return jnp.dot(a, b, preferred_element_type=f32)


def aligned(column, span, columns):
    base = jnp.minimum((column // 128) * 128, columns - span)
    return pl.multiple_of(base, 128), column - base


def crop_kernel(column_ref, spectrum_ref, out_ref):
    led_count, slots, _, double = out_ref.shape
    window = double // 2
    columns = spectrum_ref.shape[3]
    span = window + 128

    @pl.loop(0, led_count)
    def _(led):
        base, shift = aligned(column_ref[led], span, columns)
        for s in range(slots):
            for c in range(2):
                wide = spectrum_ref[c, s, :, pl.ds(base, span)].astype(f32)
                wide = pltpu.roll(wide, span - shift, 1)
                out_ref[led, s, :, c * window:(c + 1) * window] = wide[:, :window].astype(bf16)


def gradient_kernel(
    owner_ref, row_ref, strips_ref, pupil_ref, amp_ref, left_ref, right_ref, perm_ref, out_ref,
    band, psi, pupil, weight, total, used, place,
):
    led_count, slots, blk, double = strips_ref.shape
    modes, _, w, _ = pupil_ref.shape
    m = amp_ref.shape[1]
    half, h = m // 2, w // 2
    block_count = owner_ref.shape[0]
    rows = block_count * blk
    my_row = row_ref[lax.axis_index("led")]

    for n in range(led_count):
        used[n] = 0
    for b in range(block_count):
        owner = owner_ref[b]
        rank = used[owner]
        used[owner] = rank + 1
        place[b] = rank
        band[b * blk:(b + 1) * blk, :] = strips_ref[owner, rank].astype(f32)

    line = lax.broadcasted_iota(jnp.int32, (w, rows), 0)
    natural = jnp.where(line < h, 2 * line, 2 * line - w + 1)
    chosen = lax.broadcasted_iota(jnp.int32, (w, rows), 1) == natural + my_row
    chosen = jnp.where(chosen, 1.0, 0.0).astype(bf16)
    spread, gather = perm_ref[0], perm_ref[1]
    picked = dot(chosen, band[...].astype(bf16)).astype(bf16)
    xr = dot(picked[:, :w], spread)
    xi = dot(picked[:, w:], spread)

    weight[...] = jnp.zeros_like(weight)

    @pl.loop(0, modes)
    def _(k):
        parts = []
        for c in range(2):
            mixed = dot(gather, pupil_ref[k, c]).astype(bf16)
            mixed = dot(mixed, spread)
            pupil[k, c] = mixed.astype(bf16)
            parts.append(mixed)
        pr, pi = parts
        yr = (xr * pr - xi * pi).astype(bf16)
        yi = (xr * pi + xi * pr).astype(bf16)
        even = dot(jnp.concatenate([yr[:, :h], yi[:, :h]], 1), right_ref[0])
        odd = dot(jnp.concatenate([yr[:, h:], yi[:, h:]], 1), right_ref[1])
        low = (even + odd).astype(bf16)
        high = (even - odd).astype(bf16)

        def stacked(lo, hi):
            return jnp.concatenate(
                [
                    jnp.concatenate([low[lo:hi, :half], high[lo:hi, :half]], 1),
                    jnp.concatenate([low[lo:hi, half:], high[lo:hi, half:]], 1),
                ],
                0,
            )

        even = dot(left_ref[0], stacked(0, h))
        odd = dot(left_ref[1], stacked(h, w))
        top = even + odd
        bottom = even - odd
        psi[k, 0] = top
        psi[k, 1] = bottom
        weight[:half] += top[:half] * top[:half] + top[half:] * top[half:]
        weight[half:] += bottom[:half] * bottom[:half] + bottom[half:] * bottom[half:]

    modulus = jnp.sqrt(weight[...] + amp_eps)
    weight[...] = (modulus - amp_ref[0]) / modulus
    total[...] = jnp.zeros_like(total)

    @pl.loop(0, modes)
    def _(k):
        wt = weight[:half]
        wb = weight[half:]
        sums, differences = [], []
        for part in (slice(0, half), slice(half, m)):
            top = psi[k, 0, part] * wt
            bottom = psi[k, 1, part] * wb
            sums.append((top + bottom).astype(bf16))
            differences.append((top - bottom).astype(bf16))
        even = dot(right_ref[0], jnp.concatenate(sums, 0))
        odd = dot(right_ref[1], jnp.concatenate(differences, 0))
        hr = jnp.concatenate([even[:h], odd[:h]], 0)
        hi = jnp.concatenate([even[h:], odd[h:]], 0)
        plus = jnp.concatenate([hr[:, :half] + hr[:, half:], hi[:, :half] + hi[:, half:]], 1)
        minus = jnp.concatenate([hr[:, :half] - hr[:, half:], hi[:, :half] - hi[:, half:]], 1)
        even = dot(plus.astype(bf16), left_ref[0])
        odd = dot(minus.astype(bf16), left_ref[1])
        er = jnp.concatenate([even[:, :h], odd[:, :h]], 1)
        ei = jnp.concatenate([even[:, h:], odd[:, h:]], 1)
        pr = pupil[k, 0].astype(f32)
        pi = pupil[k, 1].astype(f32)
        total[0] += pr * er + pi * ei
        total[1] += pr * ei - pi * er

    sorted_back = jnp.concatenate(
        [dot(total[c].astype(bf16), gather).astype(bf16) for c in range(2)], 1
    )
    band[...] = lax.dot_general(
        chosen, sorted_back, (((0,), (0,)), ((), ())), preferred_element_type=f32
    )
    out_ref[...] = jnp.zeros_like(out_ref)
    for b in range(block_count):
        out_ref[owner_ref[b], place[b]] = band[b * blk:(b + 1) * blk, :].astype(bf16)


def add_kernel(column_ref, strips_ref, out_ref):
    led_count, slots, blk, double = strips_ref.shape
    window = double // 2
    columns = out_ref.shape[3]
    span = window + 128
    out_ref[...] = jnp.zeros_like(out_ref)

    @pl.loop(0, led_count)
    def _(led):
        base, shift = aligned(column_ref[led], span, columns)
        for s in range(slots):
            for c in range(2):
                strip = strips_ref[led, s, :, c * window:(c + 1) * window].astype(f32)
                wide = jnp.concatenate([strip, jnp.zeros((blk, 128), f32)], 1)
                out_ref[s, c, :, pl.ds(base, span)] += pltpu.roll(wide, shift, 1)


def shards(spectrum, block_owner, row_offset, column_offset, pupil_modes, amplitude):
    slots, blk, _, columns = spectrum.shape
    led_count = lax.axis_size("led")
    modes, _, w, _ = pupil_modes.shape
    m = amplitude.shape[1]
    rows = block_owner.shape[0] * blk
    left, right = dft_tables(m, w)
    perm = np.stack(deinterleave(w))
    limit = pltpu.CompilerParams(vmem_limit_bytes=50 * 1024 * 1024)
    strips_shape = jax.ShapeDtypeStruct((led_count, slots, blk, 2 * w), bf16)
    strips = pl.pallas_call(
        crop_kernel,
        out_shape=strips_shape,
        in_specs=[SMEM, VMEM],
        out_specs=VMEM,
        compiler_params=limit,
        name="crop_windows",
    )(column_offset, spectrum.transpose(2, 0, 1, 3))
    strips = lax.all_to_all(strips, "led", split_axis=0, concat_axis=0, tiled=True)
    strips = pl.pallas_call(
        gradient_kernel,
        out_shape=strips_shape,
        in_specs=[SMEM, SMEM] + [VMEM] * 6,
        out_specs=VMEM,
        scratch_shapes=[
            pltpu.VMEM((rows, 2 * w), f32),
            pltpu.VMEM((modes, 2, m, m), f32),
            pltpu.VMEM((modes, 2, w, w), bf16),
            pltpu.VMEM((m, m), f32),
            pltpu.VMEM((2, w, w), f32),
            pltpu.SMEM((led_count,), jnp.int32),
            pltpu.SMEM((block_owner.shape[0],), jnp.int32),
        ],
        compiler_params=limit,
        name="window_gradient",
    )(
        block_owner, row_offset, strips, pupil_modes, amplitude,
        jnp.asarray(left), jnp.asarray(right), jnp.asarray(perm),
    )
    strips = lax.all_to_all(strips, "led", split_axis=0, concat_axis=0, tiled=True)
    result = pl.pallas_call(
        add_kernel,
        out_shape=jax.ShapeDtypeStruct((slots, 2, blk, columns), f32),
        in_specs=[SMEM, VMEM],
        out_specs=VMEM,
        compiler_params=limit,
        name="add_strips",
    )(column_offset, strips)
    return result.transpose(0, 2, 1, 3)


def solution(mesh):
    return jax.shard_map(
        shards,
        mesh=mesh,
        in_specs=(
            P(("rep", "led"), None, None, None),
            P(),
            P(),
            P(),
            P(),
            P(("rep", "led"), None, None),
        ),
        out_specs=P(("rep", "led"), None, None, None),
        check_vma=False,
    )
```

time: 388 us -> 80.6 us (0.21)
  local copies, waits for them, and re-layouts: 156 us -> 4.9 us
  waiting for transfers between devices: 119 us -> 0 us
  blocking collectives: 0 us -> 51.8 us
  other arithmetic: 35.8 us -> 0 us
  loops' own time: 31.6 us -> 0 us
  matrix products: 24.3 us -> 0 us
  Pallas kernels: 0 us -> 23.5 us
  between operations: 15.3 us -> 0.11 us
  starting transfers between devices: 4.89 us -> 0 us
    dynamic_update_slice x16 -> x0, local copies, waits for them, and re-layouts: 133 us -> none  [add_strip(): return lax.dynamic_update_slice_in_dim(running, current + strip, start, 3)]
    all_gather x1 -> x0, waiting for transfers between devices: 86.4 us -> none  [shards(): shard_piece = lax.all_gather(spectrum, 'led', axis=0, tiled=True)]
    all_to_all x0 -> x2, blocking collectives: none -> 51.8 us  [shards(): lax.all_to_all(strips, 'led', split_axis=0, concat_axis=0, tiled=True)]
    all_to_all x1 -> x0, waiting for transfers between devices: 32.4 us -> none  [shards(): lax.all_to_all(strips_back, 'led', split_axis=0, concat_axis=0, tiled=True)]
    another operation x1 -> x0, loops' own time: 31.6 us -> none  [shards(): return lax.fori_loop(0, led_count, add_strip, result)]
    dot_general x5 -> x0, matrix products: 24.3 us -> none  [the longest x1 12.4 us: mode_gradient(): jnp.einsum('kduq,dcqv->kcuv', back_half, left_table, preferred_element_ty...]
    pallas_call x0 -> x3, Pallas kernels: none -> 23.5 us  [the longest x1 18.9 us: shards(): pl.pallas_call(gradient_kernel, out_shape=strips_shape, in_specs=[SMEM, S...]
    add x18 -> x0, other arithmetic: 17.8 us -> none  [the longest x16 17.1 us: add_strip(): return lax.dynamic_update_slice_in_dim(running, current + strip, start, 3)]
  transfers between devices with their start and end apart: 2 -> 0, of which waited for: 2 -> 0; matrix products, arithmetic and copies ran while one was open for 3% -> 0% of each run, Pallas kernels for 0% -> 0%
where the time goes in v1:
time: 80.6 us; the launch traced here: 80.3 us
  blocking collectives  51.8 us (64%)
  Pallas kernels  23.5 us (29%)
  local copies, waits for them, and re-layouts  4.9 us (6%)
    all_to_all x2, blocking collectives, shards(): lax.all_to_all(strips, 'led', split_axis=0, concat_axis=0, tiled=True)  51.8 us
    pallas_call x1, Pallas kernels, shards(): pl.pallas_call(gradient_kernel, out_shape=strips_shape, in_specs=[SMEM, S...  18.9 us
    transpose x1, local copies, waits for them, and re-layouts, shards(): return result.transpose(0, 2, 1, 3)  3.23 us
    pallas_call x1, Pallas kernels, shards(): pl.pallas_call(add_kernel, out_shape=jax.ShapeDtypeStruct((slots, 2, blk,...  2.4 us
    pallas_call x1, Pallas kernels, shards(): pl.pallas_call(crop_kernel, out_shape=strips_shape, in_specs=[SMEM, VMEM]...  2.21 us
    unnamed x15, local copies, waits for them, and re-layouts  1.67 us

profile of v1, /device:TPU:1, one launch (start us, length us, event | category | flops | bytes accessed | tf_op | source)
XLA Modules:
  0.0 80.3 jit_solution(4690277552880120554)
XLA Ops:
  0.0 0.0 copy-start.4
  0.0 1.6 %copy.13 = bf16[3,16,2,6144]{3,1,0,2:T(8,128)(2,1)S(1)} copy(bf16[3,16,2,6144]{3,2,1,0:T(2,128)(2,1)} %param.9) | data formatting | bytes 2359296 | tf_op args[0]
  1.6 0.0 copy-start
  1.6 0.0 copy-start.1
  1.7 0.0 copy-start.2
  1.7 0.0 copy-start.3
  1.7 0.0 copy-start.5
  1.7 0.0 copy-start.6
  1.7 0.0 copy-done.4
  1.7 2.2 %crop_windows.1 = bf16[16,3,16,512]{3,2,1,0:T(8,128)(2,1)S(1)} custom-call(s32[16]{0:T(128)S(1)} %copy-done.4, bf16[2,3,16,6144]{3,2,1,0:T(8,128)(2,1)S(1)} %bitcast.5), custom_call_target="tpu_custom_call" | custom-call | tf_op jit(solution)/shard_map/crop_windows/pallas_call | solution.py:201
  3.9 27.8 %all_to_all.10.strips_ref = bf16[16,3,16,512]{3,2,1,0:T(8,128)(2,1)S(1)} all-to-all(bf16[16,3,16,512]{3,2,1,0:T(8,128)(2,1)S(1)} %crop_windows.1), channel_id=1, replica_groups=mesh['rep'=2,'led'=16] {'led'}, dimensions={0} | all-to-all | bytes 1572864 | tf_op jit(solution)/shard_map/all_to_all | solution.py:209
  31.7 0.0 copy-done
  31.7 0.0 copy-done.1
  31.7 0.0 copy-done.2
  31.7 0.0 copy-done.3
  31.7 0.0 copy-done.5
  31.7 0.0 copy-done.6
  31.8 18.9 %window_gradient.1 = bf16[16,3,16,512]{3,2,1,0:T(8,128)(2,1)S(1)} custom-call(s32[24]{0:T(128)S(1)} %copy-done.5, s32[16]{0:T(128)S(1)} %copy-done.6, bf16[16,3,16,512]{3,2,1,0:T(8,128)(2,1)S(1)} %all_to_all.10.strips_ref, bf16[8,2,256,256]{3,2,1,0:T(8,128)(2,1)} %pupil_ref.1, f32[1,512,512]{2,1,0:T(8,128)S(1)} %copy-done, ...), custom_call_target="tpu_custom_call" | custom-call | tf_op jit(solution)/shard_map/window_gradient/pallas_call | solution.py:210
  50.7 24.0 %all_to_all.11.strips_ref = bf16[16,3,16,512]{3,2,1,0:T(8,128)(2,1)S(1)} all-to-all(bf16[16,3,16,512]{3,2,1,0:T(8,128)(2,1)S(1)} %window_gradient.1), channel_id=1, replica_groups=mesh['rep'=2,'led'=16] {'led'}, dimensions={0} | all-to-all | bytes 1572864 | tf_op jit(solution)/shard_map/all_to_all | solution.py:230
  74.7 2.4 %add_strips.1 = f32[3,2,16,6144]{3,2,1,0:T(8,128)S(1)} custom-call(s32[16]{0:T(128)S(1)} %copy-done.4, bf16[16,3,16,512]{3,2,1,0:T(8,128)(2,1)S(1)} %all_to_all.11.strips_ref), custom_call_target="tpu_custom_call" | custom-call | tf_op jit(solution)/shard_map/add_strips/pallas_call | solution.py:231
  77.1 3.2 %copy.11 = f32[3,16,2,6144]{3,2,1,0:T(2,128)} copy(f32[3,16,2,6144]{3,1,2,0:T(8,128)S(1)} %bitcast.4) | data formatting | bytes 4718592 | tf_op jit(solution)/shard_map/transpose | solution.py:239
Async XLA Ops:
  0.0 1.7 %copy-start.4 = (s32[16]{0:T(128)S(1)}, s32[16]{0:T(128)}, u32[]{:S(2)}) copy-start(s32[16]{0:T(128)} %column_ref.3) | copy-start | bytes 196
  1.6 30.1 %copy-start = (f32[1,512,512]{2,1,0:T(8,128)S(1)}, f32[1,512,512]{2,1,0:T(8,128)}, u32[]{:S(2)}) copy-start(f32[1,512,512]{2,1,0:T(8,128)} %amp_ref.1) | copy-start | bytes 3145732
  1.6 30.1 %copy-start.1 = (bf16[2,256,512]{2,1,0:T(8,128)(2,1)S(1)}, bf16[2,256,512]{2,1,0:T(8,128)(2,1)}, u32[]{:S(2)}) copy-start(bf16[2,256,512]{2,1,0:T(8,128)(2,1)} %constant.7.clone.right_ref) | copy-start | bytes 1572868
  1.7 30.1 %copy-start.2 = (bf16[2,512,256]{2,1,0:T(8,128)(2,1)S(1)}, bf16[2,512,256]{2,1,0:T(8,128)(2,1)}, u32[]{:S(2)}) copy-start(bf16[2,512,256]{2,1,0:T(8,128)(2,1)} %constant.6.clone.left_ref) | copy-start | bytes 1572868
  1.7 30.1 %copy-start.3 = (bf16[2,256,256]{2,1,0:T(8,128)(2,1)S(1)}, bf16[2,256,256]{2,1,0:T(8,128)(2,1)}, u32[]{:S(2)}) copy-start(bf16[2,256,256]{2,1,0:T(8,128)(2,1)} %constant.8.clone.perm_ref) | copy-start | bytes 786436
  1.7 30.0 %copy-start.5 = (s32[24]{0:T(128)S(1)}, s32[24]{0:T(128)}, u32[]{:S(2)}) copy-start(s32[24]{0:T(128)} %owner_ref.1) | copy-start | bytes 292
  1.7 30.0 %copy-start.6 = (s32[16]{0:T(128)S(1)}, s32[16]{0:T(128)}, u32[]{:S(2)}) copy-start(s32[16]{0:T(128)} %row_ref.1) | copy-start | bytes 196

commit v2 on v1

--- a/solution.py
+++ b/solution.py
@@ -14,6 +14,7 @@
 f32 = jnp.float32
 bf16 = jnp.bfloat16
 VMEM = pl.BlockSpec(memory_space=pltpu.VMEM)
+ANY = pl.BlockSpec(memory_space=pl.ANY)
 SMEM = pl.BlockSpec(memory_space=pltpu.SMEM)
 
 
@@ -49,6 +50,35 @@
     return pl.multiple_of(base, 128), column - base
 
 
+def greet(led_count, me):
+    barrier = pltpu.get_barrier_semaphore()
+
+    @pl.loop(1, led_count)
+    def _(step):
+        pl.semaphore_signal(
+            barrier, inc=1, device_id={"led": lax.rem(me + step, led_count)},
+            device_id_type=pl.DeviceIdType.MESH,
+        )
+
+    pl.semaphore_wait(barrier, led_count - 1)
+
+
+def strip_copy(step, me, led_count, source, landing, send_sem, recv_sem):
+    dest = lax.rem(me + step, led_count)
+    return pltpu.make_async_remote_copy(
+        src_ref=source.at[dest],
+        dst_ref=landing.at[me],
+        send_sem=send_sem.at[step],
+        recv_sem=recv_sem.at[step],
+        device_id={"led": dest},
+        device_id_type=pl.DeviceIdType.MESH,
+    )
+
+
+def far_first(turn, led_count):
+    return 1 + lax.rem(turn + led_count // 2 - 1, led_count - 1)
+
+
 def crop_kernel(column_ref, spectrum_ref, out_ref):
     led_count, slots, _, double = out_ref.shape
     window = double // 2
@@ -65,9 +95,55 @@
                 out_ref[led, s, :, c * window:(c + 1) * window] = wide[:, :window].astype(bf16)
 
 
+def send_kernel(
+    strips, pupil_ref, perm_ref, landing, sorted_ref, send_sem, recv_sem, own_sem,
+):
+    led_count = strips.shape[0]
+    me = lax.axis_index("led")
+    own = pltpu.make_async_copy(strips.at[me], landing.at[me], own_sem)
+    own.start()
+    greet(led_count, me)
+
+    @pl.loop(0, led_count - 1)
+    def _(turn):
+        step = far_first(turn, led_count)
+        strip_copy(step, me, led_count, strips, landing, send_sem, recv_sem).start()
+
+    @pl.loop(0, pupil_ref.shape[0])
+    def _(k):
+        for c in range(2):
+            mixed = dot(perm_ref[1], pupil_ref[k, c]).astype(bf16)
+            sorted_ref[k, c] = dot(mixed, perm_ref[0]).astype(bf16)
+
+    own.wait()
+
+    @pl.loop(1, led_count)
+    def _(step):
+        strip_copy(step, me, led_count, strips, landing, send_sem, recv_sem).wait()
+
+
+def return_kernel(strips, landing, send_sem, recv_sem, own_sem):
+    led_count = strips.shape[0]
+    me = lax.axis_index("led")
+    own = pltpu.make_async_copy(strips.at[me], landing.at[me], own_sem)
+    own.start()
+    greet(led_count, me)
+
+    @pl.loop(0, led_count - 1)
+    def _(turn):
+        step = far_first(turn, led_count)
+        strip_copy(step, me, led_count, strips, landing, send_sem, recv_sem).start()
+
+    own.wait()
+
+    @pl.loop(1, led_count)
+    def _(step):
+        strip_copy(step, me, led_count, strips, landing, send_sem, recv_sem).wait()
+
+
 def gradient_kernel(
     owner_ref, row_ref, strips_ref, pupil_ref, amp_ref, left_ref, right_ref, perm_ref, out_ref,
-    band, psi, pupil, weight, total, used, place,
+    band, psi, weight, total, used, place,
 ):
     led_count, slots, blk, double = strips_ref.shape
     modes, _, w, _ = pupil_ref.shape
@@ -99,13 +175,8 @@
 
     @pl.loop(0, modes)
     def _(k):
-        parts = []
-        for c in range(2):
-            mixed = dot(gather, pupil_ref[k, c]).astype(bf16)
-            mixed = dot(mixed, spread)
-            pupil[k, c] = mixed.astype(bf16)
-            parts.append(mixed)
-        pr, pi = parts
+        pr = pupil_ref[k, 0].astype(f32)
+        pi = pupil_ref[k, 1].astype(f32)
         yr = (xr * pr - xi * pi).astype(bf16)
         yi = (xr * pi + xi * pr).astype(bf16)
         even = dot(jnp.concatenate([yr[:, :h], yi[:, :h]], 1), right_ref[0])
@@ -155,8 +226,8 @@
         odd = dot(minus.astype(bf16), left_ref[1])
         er = jnp.concatenate([even[:, :h], odd[:, :h]], 1)
         ei = jnp.concatenate([even[:, h:], odd[:, h:]], 1)
-        pr = pupil[k, 0].astype(f32)
-        pi = pupil[k, 1].astype(f32)
+        pr = pupil_ref[k, 0].astype(f32)
+        pi = pupil_ref[k, 1].astype(f32)
         total[0] += pr * er + pi * ei
         total[1] += pr * ei - pi * er
 
@@ -171,12 +242,12 @@
         out_ref[owner_ref[b], place[b]] = band[b * blk:(b + 1) * blk, :].astype(bf16)
 
 
-def add_kernel(column_ref, strips_ref, out_ref):
+def add_kernel(column_ref, strips_ref, out_ref, total):
     led_count, slots, blk, double = strips_ref.shape
     window = double // 2
     columns = out_ref.shape[3]
     span = window + 128
-    out_ref[...] = jnp.zeros_like(out_ref)
+    total[...] = jnp.zeros_like(total)
 
     @pl.loop(0, led_count)
     def _(led):
@@ -185,7 +256,11 @@
             for c in range(2):
                 strip = strips_ref[led, s, :, c * window:(c + 1) * window].astype(f32)
                 wide = jnp.concatenate([strip, jnp.zeros((blk, 128), f32)], 1)
-                out_ref[s, c, :, pl.ds(base, span)] += pltpu.roll(wide, shift, 1)
+                total[s, c, :, pl.ds(base, span)] += pltpu.roll(wide, shift, 1)
+
+    for s in range(slots):
+        for c in range(2):
+            out_ref[s, :, c, :] = total[s, c]
 
 
 def shards(spectrum, block_owner, row_offset, column_offset, pupil_modes, amplitude):
@@ -196,17 +271,30 @@
     rows = block_owner.shape[0] * blk
     left, right = dft_tables(m, w)
     perm = np.stack(deinterleave(w))
-    limit = pltpu.CompilerParams(vmem_limit_bytes=50 * 1024 * 1024)
+    limit = functools.partial(pltpu.CompilerParams, vmem_limit_bytes=48 * 1024 * 1024)
     strips_shape = jax.ShapeDtypeStruct((led_count, slots, blk, 2 * w), bf16)
+    semaphores = [
+        pltpu.SemaphoreType.DMA((led_count,)),
+        pltpu.SemaphoreType.DMA((led_count,)),
+        pltpu.SemaphoreType.DMA,
+    ]
     strips = pl.pallas_call(
         crop_kernel,
         out_shape=strips_shape,
         in_specs=[SMEM, VMEM],
         out_specs=VMEM,
-        compiler_params=limit,
+        compiler_params=limit(),
         name="crop_windows",
     )(column_offset, spectrum.transpose(2, 0, 1, 3))
-    strips = lax.all_to_all(strips, "led", split_axis=0, concat_axis=0, tiled=True)
+    strips, pupil_sorted = pl.pallas_call(
+        send_kernel,
+        out_shape=(strips_shape, jax.ShapeDtypeStruct(pupil_modes.shape, bf16)),
+        in_specs=[ANY, VMEM, VMEM],
+        out_specs=(ANY, VMEM),
+        scratch_shapes=semaphores,
+        compiler_params=limit(collective_id=0, has_side_effects=True),
+        name="send_windows",
+    )(strips, pupil_modes, jnp.asarray(perm))
     strips = pl.pallas_call(
         gradient_kernel,
         out_shape=strips_shape,
@@ -215,28 +303,35 @@
         scratch_shapes=[
             pltpu.VMEM((rows, 2 * w), f32),
             pltpu.VMEM((modes, 2, m, m), f32),
-            pltpu.VMEM((modes, 2, w, w), bf16),
             pltpu.VMEM((m, m), f32),
             pltpu.VMEM((2, w, w), f32),
             pltpu.SMEM((led_count,), jnp.int32),
             pltpu.SMEM((block_owner.shape[0],), jnp.int32),
         ],
-        compiler_params=limit,
+        compiler_params=limit(),
         name="window_gradient",
     )(
-        block_owner, row_offset, strips, pupil_modes, amplitude,
+        block_owner, row_offset, strips, pupil_sorted, amplitude,
         jnp.asarray(left), jnp.asarray(right), jnp.asarray(perm),
     )
-    strips = lax.all_to_all(strips, "led", split_axis=0, concat_axis=0, tiled=True)
-    result = pl.pallas_call(
+    strips = pl.pallas_call(
+        return_kernel,
+        out_shape=strips_shape,
+        in_specs=[ANY],
+        out_specs=ANY,
+        scratch_shapes=semaphores,
+        compiler_params=limit(collective_id=1, has_side_effects=True),
+        name="return_strips",
+    )(strips)
+    return pl.pallas_call(
         add_kernel,
-        out_shape=jax.ShapeDtypeStruct((slots, 2, blk, columns), f32),
+        out_shape=jax.ShapeDtypeStruct((slots, blk, 2, columns), f32),
         in_specs=[SMEM, VMEM],
         out_specs=VMEM,
-        compiler_params=limit,
+        scratch_shapes=[pltpu.VMEM((slots, 2, blk, columns), f32)],
+        compiler_params=limit(),
         name="add_strips",
     )(column_offset, strips)
-    return result.transpose(0, 2, 1, 3)
 
 
 def solution(mesh):

time: 80.6 us -> 71.8 us (0.89)
  blocking collectives: 51.8 us -> 0 us
  Pallas kernels: 23.5 us -> 69.6 us
  local copies, waits for them, and re-layouts: 4.9 us -> 1.81 us
    all_to_all x2 -> x0, blocking collectives: 51.8 us -> none  [shards(): lax.all_to_all(strips, 'led', split_axis=0, concat_axis=0, tiled=True)]
    pallas_call x1 -> x3, Pallas kernels: 2.4 us -> 50.7 us  [the longest x1 24.2 us: shards(): pl.pallas_call(send_kernel, out_shape=(strips_shape, jax.ShapeDtypeStruct...]
    transpose x1 -> x0, local copies, waits for them, and re-layouts: 3.23 us -> none  [shards(): return result.transpose(0, 2, 1, 3)]
    pallas_call x1, Pallas kernels: 18.9 us -> 16.7 us  [shards(): pl.pallas_call(gradient_kernel, out_shape=strips_shape, in_specs=[SMEM, S...]
    unnamed x15 -> x17, local copies, waits for them, and re-layouts: 1.67 us -> 1.81 us
where the time goes in v2:
time: 71.8 us; the launch traced here: 71.6 us
  Pallas kernels  69.6 us (97%)
  local copies, waits for them, and re-layouts  1.81 us (3%)
    pallas_call x1, Pallas kernels, shards(): pl.pallas_call(send_kernel, out_shape=(strips_shape, jax.ShapeDtypeStruct...  24.2 us
    pallas_call x1, Pallas kernels, shards(): pl.pallas_call(return_kernel, out_shape=strips_shape, in_specs=[ANY], out...  22.3 us
    pallas_call x1, Pallas kernels, shards(): pl.pallas_call(gradient_kernel, out_shape=strips_shape, in_specs=[SMEM, S...  16.7 us
    pallas_call x1, Pallas kernels, shards(): pl.pallas_call(add_kernel, out_shape=jax.ShapeDtypeStruct((slots, blk, 2,...  4.2 us
    pallas_call x1, Pallas kernels, shards(): pl.pallas_call(crop_kernel, out_shape=strips_shape, in_specs=[SMEM, VMEM]...  2.21 us
    unnamed x17, local copies, waits for them, and re-layouts  1.81 us

profile of v2, /device:TPU:1, one launch (start us, length us, event | category | flops | bytes accessed | tf_op | source)
XLA Modules:
  0.0 71.6 jit_solution(2549816387930723076)
XLA Ops:
  0.0 0.0 copy-start.2
  0.0 0.0 copy-start.5
  0.0 0.0 copy-start
  0.0 1.8 %copy.12 = bf16[3,16,2,6144]{3,1,0,2:T(8,128)(2,1)S(1)} copy(bf16[3,16,2,6144]{3,2,1,0:T(2,128)(2,1)} %param.9) | data formatting | bytes 2359296 | tf_op args[0]
  1.8 0.0 copy-done.5
  1.8 0.0 copy-start.1
  1.8 0.0 copy-start.3
  1.8 0.0 copy-start.4
  1.8 0.0 copy-start.6
  1.8 0.0 copy-start.7
  1.9 2.2 %crop_windows.1.strips = bf16[16,3,16,512]{3,2,1,0:T(8,128)(2,1)S(1)} custom-call(s32[16]{0:T(128)S(1)} %copy-done.5, bf16[2,3,16,6144]{3,2,1,0:T(8,128)(2,1)S(1)} %bitcast.3), custom_call_target="tpu_custom_call" | custom-call | tf_op jit(solution)/shard_map/crop_windows/pallas_call | solution.py:281
  4.1 0.0 copy-done.2
  4.1 0.0 copy-done
  4.1 24.2 %send_windows.1 = (bf16[16,3,16,512]{3,2,1,0:T(8,128)(2,1)S(1)}, bf16[8,2,256,256]{3,2,1,0:T(8,128)(2,1)S(1)}) custom-call(bf16[16,3,16,512]{3,2,1,0:T(8,128)(2,1)S(1)} %crop_windows.1.strips, bf16[8,2,256,256]{3,2,1,0:T(8,128)(2,1)S(1)} %copy-done, bf16[2,256,256]{2,1,0:T(8,128)(2,1)S(1)} %copy-done.2), custom_call_target="tpu_custom_call" | custom-call | tf_op jit(solution)/shard_map/send_windows/pallas_call | solution.py:289
  28.3 0.0 copy-done.1
  28.3 0.0 copy-done.3
  28.3 0.0 copy-done.4
  28.3 0.0 copy-done.6
  28.3 0.0 copy-done.7
  28.3 16.7 %window_gradient.1.strips = bf16[16,3,16,512]{3,2,1,0:T(8,128)(2,1)S(1)} custom-call(s32[24]{0:T(128)S(1)} %copy-done.6, s32[16]{0:T(128)S(1)} %copy-done.7, bf16[16,3,16,512]{3,2,1,0:T(8,128)(2,1)S(1)} %get-tuple-element.7.strips_ref, bf16[8,2,256,256]{3,2,1,0:T(8,128)(2,1)S(1)} %get-tuple-element.8.pupil_ref, f32[1,512,512]{2,1,0:T(8,128)S(1)} %copy-done.1, ...), custom_call_target="tpu_custom_call" | custom-call | tf_op jit(solution)/shard_map/window_gradient/pallas_call | solution.py:298
  45.0 22.3 %return_strips.1.strips_ref = bf16[16,3,16,512]{3,2,1,0:T(8,128)(2,1)S(1)} custom-call(bf16[16,3,16,512]{3,2,1,0:T(8,128)(2,1)S(1)} %window_gradient.1.strips), custom_call_target="tpu_custom_call" | custom-call | tf_op jit(solution)/shard_map/return_strips/pallas_call | solution.py:317
  67.4 4.2 %add_strips.1 = f32[3,16,2,6144]{3,2,1,0:T(2,128)} custom-call(s32[16]{0:T(128)S(1)} %copy-done.5, bf16[16,3,16,512]{3,2,1,0:T(8,128)(2,1)S(1)} %return_strips.1.strips_ref), custom_call_target="tpu_custom_call" | custom-call | tf_op jit(solution)/shard_map/add_strips/pallas_call | solution.py:326
Async XLA Ops:
  0.0 4.1 %copy-start.2 = (bf16[2,256,256]{2,1,0:T(8,128)(2,1)S(1)}, bf16[2,256,256]{2,1,0:T(8,128)(2,1)}, u32[]{:S(2)}) copy-start(bf16[2,256,256]{2,1,0:T(8,128)(2,1)} %constant.6.clone.perm_ref) | copy-start | bytes 786436
  0.0 1.8 %copy-start.5 = (s32[16]{0:T(128)S(1)}, s32[16]{0:T(128)}, u32[]{:S(2)}) copy-start(s32[16]{0:T(128)} %column_ref.3) | copy-start | bytes 196
  0.0 4.1 %copy-start = (bf16[8,2,256,256]{3,2,1,0:T(8,128)(2,1)S(1)}, bf16[8,2,256,256]{3,2,1,0:T(8,128)(2,1)}, u32[]{:S(2)}) copy-start(bf16[8,2,256,256]{3,2,1,0:T(8,128)(2,1)} %pupil_ref.1) | copy-start | bytes 6291460
  1.8 26.5 %copy-start.1 = (f32[1,512,512]{2,1,0:T(8,128)S(1)}, f32[1,512,512]{2,1,0:T(8,128)}, u32[]{:S(2)}) copy-start(f32[1,512,512]{2,1,0:T(8,128)} %amp_ref.1) | copy-start | bytes 3145732
  1.8 26.5 %copy-start.3 = (bf16[2,256,512]{2,1,0:T(8,128)(2,1)S(1)}, bf16[2,256,512]{2,1,0:T(8,128)(2,1)}, u32[]{:S(2)}) copy-start(bf16[2,256,512]{2,1,0:T(8,128)(2,1)} %constant.8.clone.right_ref) | copy-start | bytes 1572868
  1.8 26.5 %copy-start.4 = (bf16[2,512,256]{2,1,0:T(8,128)(2,1)S(1)}, bf16[2,512,256]{2,1,0:T(8,128)(2,1)}, u32[]{:S(2)}) copy-start(bf16[2,512,256]{2,1,0:T(8,128)(2,1)} %constant.7.clone.left_ref) | copy-start | bytes 1572868
  1.8 26.5 %copy-start.6 = (s32[24]{0:T(128)S(1)}, s32[24]{0:T(128)}, u32[]{:S(2)}) copy-start(s32[24]{0:T(128)} %owner_ref.1) | copy-start | bytes 292
  1.8 26.5 %copy-start.7 = (s32[16]{0:T(128)S(1)}, s32[16]{0:T(128)}, u32[]{:S(2)}) copy-start(s32[16]{0:T(128)} %row_ref.1) | copy-start | bytes 196

commit v3 on v1

v3 whole, which is shorter than its diff:
```python
import functools
import math

import jax
import jax.numpy as jnp
import ml_dtypes
import numpy as np
from jax import lax
from jax.experimental import pallas as pl
from jax.experimental.pallas import tpu as pltpu
from jax.sharding import PartitionSpec as P

amp_eps = 0.1
f32 = jnp.float32
bf16 = jnp.bfloat16
VMEM = pl.BlockSpec(memory_space=pltpu.VMEM)
ANY = pl.BlockSpec(memory_space=pl.ANY)
SMEM = pl.BlockSpec(memory_space=pltpu.SMEM)


def dft_tables(image_side, window_side):
    half = image_side // 2
    pixel = np.arange(half, dtype=np.int64)[:, None]
    freq = np.arange(window_side, dtype=np.int64)[None, :] - window_side // 2
    phase = np.mod(pixel * freq, image_side).astype(np.float64) * (2.0 * math.pi / image_side)
    scale = 1.0 / math.sqrt(image_side)
    real = (np.cos(phase) * scale).astype(np.float32).astype(ml_dtypes.bfloat16)
    imag = (np.sin(phase) * scale).astype(np.float32).astype(ml_dtypes.bfloat16)
    left = []
    for parity in (0, 1):
        a, b = real[:, parity::2], imag[:, parity::2]
        left.append(np.block([[a, -b], [b, a]]))
    left = np.stack(left)
    right = np.ascontiguousarray(left.transpose(0, 2, 1))
    return left, right


def deinterleave(side):
    order = np.concatenate([np.arange(0, side, 2), np.arange(1, side, 2)])
    perm = (np.arange(side)[:, None] == order[None, :]).astype(ml_dtypes.bfloat16)
    return perm, np.ascontiguousarray(perm.T)


def dot(a, b):
    return jnp.dot(a, b, preferred_element_type=f32)


def aligned(column, span, columns):
    base = jnp.minimum((column // 128) * 128, columns - span)
    return pl.multiple_of(base, 128), column - base


def greet(led_count, me):
    barrier = pltpu.get_barrier_semaphore()

    @pl.loop(1, led_count)
    def _(step):
        pl.semaphore_signal(
            barrier, inc=1, device_id={"led": lax.rem(me + step, led_count)},
            device_id_type=pl.DeviceIdType.MESH,
        )

    pl.semaphore_wait(barrier, led_count - 1)


def strip_copy(step, me, led_count, source, landing, send_sem, recv_sem):
    dest = lax.rem(me + step, led_count)
    return pltpu.make_async_remote_copy(
        src_ref=source.at[dest],
        dst_ref=landing.at[me],
        send_sem=send_sem.at[step],
        recv_sem=recv_sem.at[step],
        device_id={"led": dest},
        device_id_type=pl.DeviceIdType.MESH,
    )


def far_first(turn, led_count):
    return 1 + lax.rem(turn + led_count // 2 - 1, led_count - 1)


def crop_kernel(owner_ref, row_ref, column_ref, spectrum_ref, out_ref, line_ref, used):
    led_count, depth, double = out_ref.shape
    _, slots, blk, columns = spectrum_ref.shape
    window = double // 2
    span = window + 128
    if depth > slots * blk:
        out_ref[...] = jnp.zeros_like(out_ref)

    @pl.loop(0, led_count)
    def _(led):
        base, shift = aligned(column_ref[led], span, columns)
        for s in range(slots):
            for c in range(2):
                wide = spectrum_ref[c, s, :, pl.ds(base, span)].astype(f32)
                wide = pltpu.roll(wide, span - shift, 1)
                out_ref[led, s * blk:(s + 1) * blk, c * window:(c + 1) * window] = (
                    wide[:, :window].astype(bf16)
                )

    my_row = row_ref[lax.axis_index("led")]
    for n in range(led_count):
        used[n] = 0
    place = lax.broadcasted_iota(jnp.int32, line_ref.shape, 1)
    line = jnp.full(line_ref.shape, -1, jnp.int32)
    for b in range(owner_ref.shape[0]):
        owner = owner_ref[b]
        rank = used[owner]
        used[owner] = rank + 1
        inside = place - (owner * depth + rank * blk)
        line = jnp.where((inside >= 0) & (inside < blk), inside + (b * blk - my_row), line)
    line_ref[...] = line


def gradient_kernel(
    line_ref, strips, pupil_ref, amp_ref, left_ref, right_ref, perm_ref, returned,
    arrived, leaving, chosen, chosen_back, psi, pupil, weight, total,
    send_sem, recv_sem, back_send_sem, back_recv_sem, own_sem,
):
    led_count, depth, double = strips.shape
    modes, _, w, _ = pupil_ref.shape
    m = amp_ref.shape[1]
    half, h = m // 2, w // 2
    rows = led_count * depth
    me = lax.axis_index("led")

    def exchange(source, landing, sends, recvs, beside):
        own = pltpu.make_async_copy(source.at[me], landing.at[me], own_sem)
        own.start()

        @pl.loop(0, led_count - 1)
        def _(turn):
            step = far_first(turn, led_count)
            strip_copy(step, me, led_count, source, landing, sends, recvs).start()

        beside()
        own.wait()

        @pl.loop(1, led_count)
        def _(step):
            strip_copy(step, me, led_count, source, landing, sends, recvs).wait()

    spread, gather = perm_ref[0], perm_ref[1]

    def prepare():
        place = lax.broadcasted_iota(jnp.int32, (w, rows), 0)
        natural = jnp.where(place < h, 2 * place, 2 * place - w + 1)
        picks = jnp.where(line_ref[0:1] == natural, 1.0, 0.0)
        chosen[...] = picks.astype(bf16)
        chosen_back[...] = picks.T.astype(bf16)

        @pl.loop(0, modes)
        def _(k):
            for c in range(2):
                mixed = dot(perm_ref[1], pupil_ref[k, c]).astype(bf16)
                pupil[k, c] = dot(mixed, perm_ref[0])

        weight[...] = jnp.zeros_like(weight)
        total[...] = jnp.zeros_like(total)

    greet(led_count, me)
    exchange(strips, arrived, send_sem, recv_sem, prepare)

    picked = dot(chosen[...], arrived[...].reshape(rows, double)).astype(bf16)
    xr = dot(picked[:, :w], spread)
    xi = dot(picked[:, w:], spread)

    @pl.loop(0, modes)
    def _(k):
        pr = pupil[k, 0]
        pi = pupil[k, 1]
        yr = (xr * pr - xi * pi).astype(bf16)
        yi = (xr * pi + xi * pr).astype(bf16)
        even = dot(jnp.concatenate([yr[:, :h], yi[:, :h]], 1), right_ref[0])
        odd = dot(jnp.concatenate([yr[:, h:], yi[:, h:]], 1), right_ref[1])
        low = (even + odd).astype(bf16)
        high = (even - odd).astype(bf16)

        def stacked(lo, hi):
            return jnp.concatenate(
                [
                    jnp.concatenate([low[lo:hi, :half], high[lo:hi, :half]], 1),
                    jnp.concatenate([low[lo:hi, half:], high[lo:hi, half:]], 1),
                ],
                0,
            )

        even = dot(left_ref[0], stacked(0, h))
        odd = dot(left_ref[1], stacked(h, w))
        top = even + odd
        bottom = even - odd
        psi[k, 0] = top
        psi[k, 1] = bottom
        weight[:half] += top[:half] * top[:half] + top[half:] * top[half:]
        weight[half:] += bottom[:half] * bottom[:half] + bottom[half:] * bottom[half:]

    modulus = jnp.sqrt(weight[...] + amp_eps)
    weight[...] = (modulus - amp_ref[0]) / modulus

    @pl.loop(0, modes)
    def _(k):
        wt = weight[:half]
        wb = weight[half:]
        sums, differences = [], []
        for part in (slice(0, half), slice(half, m)):
            top = psi[k, 0, part] * wt
            bottom = psi[k, 1, part] * wb
            sums.append((top + bottom).astype(bf16))
            differences.append((top - bottom).astype(bf16))
        even = dot(right_ref[0], jnp.concatenate(sums, 0))
        odd = dot(right_ref[1], jnp.concatenate(differences, 0))
        hr = jnp.concatenate([even[:h], odd[:h]], 0)
        hi = jnp.concatenate([even[h:], odd[h:]], 0)
        plus = jnp.concatenate([hr[:, :half] + hr[:, half:], hi[:, :half] + hi[:, half:]], 1)
        minus = jnp.concatenate([hr[:, :half] - hr[:, half:], hi[:, :half] - hi[:, half:]], 1)
        even = dot(plus.astype(bf16), left_ref[0])
        odd = dot(minus.astype(bf16), left_ref[1])
        er = jnp.concatenate([even[:, :h], odd[:, :h]], 1)
        ei = jnp.concatenate([even[:, h:], odd[:, h:]], 1)
        pr = pupil[k, 0]
        pi = pupil[k, 1]
        total[0] += pr * er + pi * ei
        total[1] += pr * ei - pi * er

    sorted_back = jnp.concatenate(
        [dot(total[c].astype(bf16), gather).astype(bf16) for c in range(2)], 1
    )
    leaving[...] = dot(chosen_back[...], sorted_back).astype(bf16).reshape(leaving.shape)
    exchange(leaving, returned, back_send_sem, back_recv_sem, lambda: None)


def add_kernel(column_ref, strips_ref, out_ref, total):
    led_count, _, double = strips_ref.shape
    slots, blk, _, columns = out_ref.shape
    window = double // 2
    span = window + 128
    total[...] = jnp.zeros_like(total)

    @pl.loop(0, led_count)
    def _(led):
        base, shift = aligned(column_ref[led], span, columns)
        for s in range(slots):
            for c in range(2):
                strip = strips_ref[led, s * blk:(s + 1) * blk, c * window:(c + 1) * window]
                strip = strip.astype(f32)
                wide = jnp.concatenate([strip, jnp.zeros((blk, 128), f32)], 1)
                total[s, c, :, pl.ds(base, span)] += pltpu.roll(wide, shift, 1)

    for s in range(slots):
        for c in range(2):
            out_ref[s, :, c, :] = total[s, c]


def shards(spectrum, block_owner, row_offset, column_offset, pupil_modes, amplitude):
    slots, blk, _, columns = spectrum.shape
    led_count = lax.axis_size("led")
    modes, _, w, _ = pupil_modes.shape
    m = amplitude.shape[1]
    depth = -(-slots * blk // 16) * 16
    rows = led_count * depth
    left, right = dft_tables(m, w)
    perm = np.stack(deinterleave(w))
    limit = functools.partial(pltpu.CompilerParams, vmem_limit_bytes=48 * 1024 * 1024)
    strips_shape = jax.ShapeDtypeStruct((led_count, depth, 2 * w), bf16)
    strips, line = pl.pallas_call(
        crop_kernel,
        out_shape=(strips_shape, jax.ShapeDtypeStruct((8, rows), jnp.int32)),
        in_specs=[SMEM, SMEM, SMEM, VMEM],
        out_specs=(VMEM, VMEM),
        scratch_shapes=[pltpu.SMEM((led_count,), jnp.int32)],
        compiler_params=limit(),
        name="crop_windows",
    )(block_owner, row_offset, column_offset, spectrum.transpose(2, 0, 1, 3))
    strips = pl.pallas_call(
        gradient_kernel,
        out_shape=strips_shape,
        in_specs=[VMEM, ANY] + [VMEM] * 5,
        out_specs=ANY,
        scratch_shapes=[
            pltpu.VMEM(strips_shape.shape, bf16),
            pltpu.VMEM(strips_shape.shape, bf16),
            pltpu.VMEM((w, rows), bf16),
            pltpu.VMEM((rows, w), bf16),
            pltpu.VMEM((modes, 2, m, m), f32),
            pltpu.VMEM((modes, 2, w, w), f32),
            pltpu.VMEM((m, m), f32),
            pltpu.VMEM((2, w, w), f32),
            pltpu.SemaphoreType.DMA((led_count,)),
            pltpu.SemaphoreType.DMA((led_count,)),
            pltpu.SemaphoreType.DMA((led_count,)),
            pltpu.SemaphoreType.DMA((led_count,)),
            pltpu.SemaphoreType.DMA,
        ],
        compiler_params=limit(collective_id=0, has_side_effects=True),
        name="window_gradient",
    )(
        line, strips, pupil_modes, amplitude,
        jnp.asarray(left), jnp.asarray(right), jnp.asarray(perm),
    )
    return pl.pallas_call(
        add_kernel,
        out_shape=jax.ShapeDtypeStruct((slots, blk, 2, columns), f32),
        in_specs=[SMEM, VMEM],
        out_specs=VMEM,
        scratch_shapes=[pltpu.VMEM((slots, 2, blk, columns), f32)],
        compiler_params=limit(),
        name="add_strips",
    )(column_offset, strips)


def solution(mesh):
    return jax.shard_map(
        shards,
        mesh=mesh,
        in_specs=(
            P(("rep", "led"), None, None, None),
            P(),
            P(),
            P(),
            P(),
            P(("rep", "led"), None, None),
        ),
        out_specs=P(("rep", "led"), None, None, None),
        check_vma=False,
    )
```

time: 80.6 us -> 71.8 us (0.89)
  blocking collectives: 51.8 us -> 0 us
  Pallas kernels: 23.5 us -> 66.4 us
    all_to_all x2 -> x0, blocking collectives: 51.8 us -> none  [shards(): lax.all_to_all(strips, 'led', split_axis=0, concat_axis=0, tiled=True)]
    pallas_call x3, Pallas kernels: 23.5 us -> 66.4 us  [the longest x1 59.8 us: shards(): pl.pallas_call(gradient_kernel, out_shape=strips_shape, in_specs=[VMEM, A...]
    unnamed x15 -> x17, local copies, waits for them, and re-layouts: 1.67 us -> 5.17 us
    transpose x1 -> x0, local copies, waits for them, and re-layouts: 3.23 us -> none  [shards(): return result.transpose(0, 2, 1, 3)]
where the time goes in v3:
time: 71.8 us; the launch traced here: 71.6 us
  Pallas kernels  66.4 us (92%)
  local copies, waits for them, and re-layouts  5.17 us (7%)
    pallas_call x1, Pallas kernels, shards(): pl.pallas_call(gradient_kernel, out_shape=strips_shape, in_specs=[VMEM, A...  59.8 us
    unnamed x17, local copies, waits for them, and re-layouts  5.17 us
    pallas_call x1, Pallas kernels, shards(): pl.pallas_call(add_kernel, out_shape=jax.ShapeDtypeStruct((slots, blk, 2,...  4.2 us
    pallas_call x1, Pallas kernels, shards(): pl.pallas_call(crop_kernel, out_shape=(strips_shape, jax.ShapeDtypeStruct...  2.36 us

profile of v3, /device:TPU:1, one launch (start us, length us, event | category | flops | bytes accessed | tf_op | source)
XLA Modules:
  0.0 71.6 jit_solution(8038267101137916409)
XLA Ops:
  0.0 0.0 copy-start.4
  0.0 0.0 copy-start.5
  0.0 0.0 copy-start.1
  0.0 0.0 copy-start
  0.0 1.8 %copy.12 = bf16[3,16,2,6144]{3,1,0,2:T(8,128)(2,1)S(1)} copy(bf16[3,16,2,6144]{3,2,1,0:T(2,128)(2,1)} %param.9) | data formatting | bytes 2359296 | tf_op args[0]
  1.8 0.0 copy-done.5
  1.8 0.0 copy-start.6
  1.8 0.6 copy-done.6
  2.5 0.0 copy-start.7
  2.5 0.7 copy-done.7
  3.1 2.4 %crop_windows.1 = (bf16[16,48,512]{2,1,0:T(8,128)(2,1)S(1)}, s32[8,768]{1,0:T(8,128)S(1)}) custom-call(s32[24]{0:T(128)S(1)} %copy-done.6, s32[16]{0:T(128)S(1)} %copy-done.7, s32[16]{0:T(128)S(1)} %copy-done.5, bf16[2,3,16,6144]{3,2,1,0:T(8,128)(2,1)S(1)} %bitcast.3), custom_call_target="tpu_custom_call" | custom-call | tf_op jit(solution)/shard_map/crop_windows/pallas_call | solution.py:265
  5.5 0.0 copy-done.4
  5.5 0.0 copy-done.1
  5.5 0.0 copy-done
  5.5 0.0 copy-start.2
  5.5 1.0 %copy-done.2 = bf16[2,256,512]{2,1,0:T(8,128)(2,1)S(1)} copy-done((bf16[2,256,512]{2,1,0:T(8,128)(2,1)S(1)}, bf16[2,256,512]{2,1,0:T(8,128)(2,1)}, u32[]{:S(2)}) %copy-start.2) | copy-done | bytes 524312
  6.6 0.0 copy-start.3
  6.6 1.0 %copy-done.3 = bf16[2,512,256]{2,1,0:T(8,128)(2,1)S(1)} copy-done((bf16[2,512,256]{2,1,0:T(8,128)(2,1)S(1)}, bf16[2,512,256]{2,1,0:T(8,128)(2,1)}, u32[]{:S(2)}) %copy-start.3) | copy-done | bytes 524312
  7.6 59.8 %window_gradient.1.strips_ref = bf16[16,48,512]{2,1,0:T(8,128)(2,1)S(1)} custom-call(s32[8,768]{1,0:T(8,128)S(1)} %get-tuple-element.7.line_ref, bf16[16,48,512]{2,1,0:T(8,128)(2,1)S(1)} %get-tuple-element.8.strips, bf16[8,2,256,256]{3,2,1,0:T(8,128)(2,1)S(1)} %copy-done, f32[1,512,512]{2,1,0:T(8,128)S(1)} %copy-done.1, bf16[2,512,256]{2,1,0:T(8,128)(2,1)S(1)} %copy-done.3, ...), custom_call_target="tpu_custom_call" | custom-call | tf_op jit(solution)/shard_map/window_gradient/pallas_call | solution.py:274
  67.4 4.2 %add_strips.1 = f32[3,16,2,6144]{3,2,1,0:T(2,128)} custom-call(s32[16]{0:T(128)S(1)} %copy-done.5, bf16[16,48,512]{2,1,0:T(8,128)(2,1)S(1)} %window_gradient.1.strips_ref), custom_call_target="tpu_custom_call" | custom-call | tf_op jit(solution)/shard_map/add_strips/pallas_call | solution.py:300
Async XLA Ops:
  0.0 5.5 %copy-start.4 = (bf16[2,256,256]{2,1,0:T(8,128)(2,1)S(1)}, bf16[2,256,256]{2,1,0:T(8,128)(2,1)}, u32[]{:S(2)}) copy-start(bf16[2,256,256]{2,1,0:T(8,128)(2,1)} %constant.8.clone.perm_ref) | copy-start | bytes 786436
  0.0 1.8 %copy-start.5 = (s32[16]{0:T(128)S(1)}, s32[16]{0:T(128)}, u32[]{:S(2)}) copy-start(s32[16]{0:T(128)} %column_ref.3) | copy-start | bytes 196
  0.0 5.5 %copy-start.1 = (f32[1,512,512]{2,1,0:T(8,128)S(1)}, f32[1,512,512]{2,1,0:T(8,128)}, u32[]{:S(2)}) copy-start(f32[1,512,512]{2,1,0:T(8,128)} %amp_ref.1) | copy-start | bytes 3145732
  0.0 5.5 %copy-start = (bf16[8,2,256,256]{3,2,1,0:T(8,128)(2,1)S(1)}, bf16[8,2,256,256]{3,2,1,0:T(8,128)(2,1)}, u32[]{:S(2)}) copy-start(bf16[8,2,256,256]{3,2,1,0:T(8,128)(2,1)} %pupil_ref.1) | copy-start | bytes 6291460
  1.8 0.7 copy-start.6
  2.5 0.7 copy-start.7
  5.5 1.0 %copy-start.2 = (bf16[2,256,512]{2,1,0:T(8,128)(2,1)S(1)}, bf16[2,256,512]{2,1,0:T(8,128)(2,1)}, u32[]{:S(2)}) copy-start(bf16[2,256,512]{2,1,0:T(8,128)(2,1)} %constant.7.clone.right_ref) | copy-start | bytes 1572868
  6.6 1.0 %copy-start.3 = (bf16[2,512,256]{2,1,0:T(8,128)(2,1)S(1)}, bf16[2,512,256]{2,1,0:T(8,128)(2,1)}, u32[]{:S(2)}) copy-start(bf16[2,512,256]{2,1,0:T(8,128)(2,1)} %constant.6.clone.left_ref) | copy-start | bytes 1572868

commit v4 on v3

--- a/solution.py
+++ b/solution.py
@@ -79,24 +79,24 @@
     return 1 + lax.rem(turn + led_count // 2 - 1, led_count - 1)
 
 
-def crop_kernel(owner_ref, row_ref, column_ref, spectrum_ref, out_ref, line_ref, used):
+def crop_kernel(
+    slots, owner_ref, row_ref, column_ref, spectrum_ref, out_ref, line_ref, used,
+):
     led_count, depth, double = out_ref.shape
-    _, slots, blk, columns = spectrum_ref.shape
+    rows, columns = spectrum_ref.shape
+    height = rows // 2
+    blk = height // slots
     window = double // 2
     span = window + 128
-    if depth > slots * blk:
+    if depth > height:
         out_ref[...] = jnp.zeros_like(out_ref)
 
-    @pl.loop(0, led_count)
+    @pl.loop(0, led_count, unroll=4)
     def _(led):
         base, shift = aligned(column_ref[led], span, columns)
-        for s in range(slots):
-            for c in range(2):
-                wide = spectrum_ref[c, s, :, pl.ds(base, span)].astype(f32)
-                wide = pltpu.roll(wide, span - shift, 1)
-                out_ref[led, s * blk:(s + 1) * blk, c * window:(c + 1) * window] = (
-                    wide[:, :window].astype(bf16)
-                )
+        wide = pltpu.roll(spectrum_ref[:, pl.ds(base, span)].astype(f32), span - shift, 1)
+        wide = jnp.concatenate([wide[:height, :window], wide[height:, :window]], 1)
+        out_ref[led, :height, :] = wide.astype(bf16)
 
     my_row = row_ref[lax.axis_index("led")]
     for n in range(led_count):
@@ -113,9 +113,9 @@
 
 
 def gradient_kernel(
-    line_ref, strips, pupil_ref, amp_ref, left_ref, right_ref, perm_ref, returned,
-    arrived, leaving, chosen, chosen_back, psi, pupil, weight, total,
-    send_sem, recv_sem, back_send_sem, back_recv_sem, own_sem,
+    line_ref, strips, pupil_hbm, amp_hbm, left_hbm, right_hbm, perm_hbm, returned,
+    pupil_ref, amp_ref, left_ref, right_ref, perm_ref, arrived, leaving, chosen, chosen_back, psi, pupil, weight, total,
+    send_sem, recv_sem, back_send_sem, back_recv_sem, own_sem, load_sem,
 ):
     led_count, depth, double = strips.shape
     modes, _, w, _ = pupil_ref.shape
@@ -140,15 +140,28 @@
         def _(step):
             strip_copy(step, me, led_count, source, landing, sends, recvs).wait()
 
-    spread, gather = perm_ref[0], perm_ref[1]
+    loads = [
+        pltpu.make_async_copy(source, target, load_sem.at[n])
+        for n, (source, target) in enumerate(
+            [
+                (perm_hbm, perm_ref), (pupil_hbm, pupil_ref), (amp_hbm, amp_ref),
+                (left_hbm, left_ref), (right_hbm, right_ref),
+            ]
+        )
+    ]
 
     def prepare():
+        for load in loads:
+            load.start()
         place = lax.broadcasted_iota(jnp.int32, (w, rows), 0)
         natural = jnp.where(place < h, 2 * place, 2 * place - w + 1)
         picks = jnp.where(line_ref[0:1] == natural, 1.0, 0.0)
         chosen[...] = picks.astype(bf16)
         chosen_back[...] = picks.T.astype(bf16)
 
+        for load in loads:
+            load.wait()
+
         @pl.loop(0, modes)
         def _(k):
             for c in range(2):
@@ -161,11 +174,12 @@
     greet(led_count, me)
     exchange(strips, arrived, send_sem, recv_sem, prepare)
 
+    spread, gather = perm_ref[0], perm_ref[1]
     picked = dot(chosen[...], arrived[...].reshape(rows, double)).astype(bf16)
     xr = dot(picked[:, :w], spread)
     xi = dot(picked[:, w:], spread)
 
-    @pl.loop(0, modes)
+    @pl.loop(0, modes, unroll=modes)
     def _(k):
         pr = pupil[k, 0]
         pi = pupil[k, 1]
@@ -197,7 +211,7 @@
     modulus = jnp.sqrt(weight[...] + amp_eps)
     weight[...] = (modulus - amp_ref[0]) / modulus
 
-    @pl.loop(0, modes)
+    @pl.loop(0, modes, unroll=modes)
     def _(k):
         wt = weight[:half]
         wb = weight[half:]
@@ -229,26 +243,30 @@
     exchange(leaving, returned, back_send_sem, back_recv_sem, lambda: None)
 
 
-def add_kernel(column_ref, strips_ref, out_ref, total):
-    led_count, _, double = strips_ref.shape
+def add_kernel(column_ref, strips_ref, out_hbm, total, out_ref, out_sem):
+    led_count, depth, double = strips_ref.shape
     slots, blk, _, columns = out_ref.shape
     window = double // 2
     span = window + 128
     total[...] = jnp.zeros_like(total)
 
-    @pl.loop(0, led_count)
+    @pl.loop(0, led_count, unroll=4)
     def _(led):
         base, shift = aligned(column_ref[led], span, columns)
-        for s in range(slots):
-            for c in range(2):
-                strip = strips_ref[led, s * blk:(s + 1) * blk, c * window:(c + 1) * window]
-                strip = strip.astype(f32)
-                wide = jnp.concatenate([strip, jnp.zeros((blk, 128), f32)], 1)
-                total[s, c, :, pl.ds(base, span)] += pltpu.roll(wide, shift, 1)
-
+        strip = strips_ref[led].astype(f32)
+        strip = jnp.concatenate([strip[:, :window], strip[:, window:]], 0)
+        wide = jnp.concatenate([strip, jnp.zeros((2 * depth, 128), f32)], 1)
+        total[:, pl.ds(base, span)] += pltpu.roll(wide, shift, 1)
+
+    copies = []
     for s in range(slots):
         for c in range(2):
-            out_ref[s, :, c, :] = total[s, c]
+            first = c * depth + s * blk
+            out_ref[s, :, c, :] = total[first:first + blk, :]
+        copies.append(pltpu.make_async_copy(out_ref.at[s], out_hbm.at[s], out_sem.at[s]))
+        copies[-1].start()
+    for copy in copies:
+        copy.wait()
 
 
 def shards(spectrum, block_owner, row_offset, column_offset, pupil_modes, amplitude):
@@ -260,23 +278,28 @@
     rows = led_count * depth
     left, right = dft_tables(m, w)
     perm = np.stack(deinterleave(w))
-    limit = functools.partial(pltpu.CompilerParams, vmem_limit_bytes=48 * 1024 * 1024)
+    limit = functools.partial(pltpu.CompilerParams, vmem_limit_bytes=60 * 1024 * 1024)
     strips_shape = jax.ShapeDtypeStruct((led_count, depth, 2 * w), bf16)
     strips, line = pl.pallas_call(
-        crop_kernel,
+        functools.partial(crop_kernel, slots),
         out_shape=(strips_shape, jax.ShapeDtypeStruct((8, rows), jnp.int32)),
         in_specs=[SMEM, SMEM, SMEM, VMEM],
         out_specs=(VMEM, VMEM),
         scratch_shapes=[pltpu.SMEM((led_count,), jnp.int32)],
-        compiler_params=limit(),
+        compiler_params=pltpu.CompilerParams(vmem_limit_bytes=48 * 1024 * 1024),
         name="crop_windows",
-    )(block_owner, row_offset, column_offset, spectrum.transpose(2, 0, 1, 3))
+    )(block_owner, row_offset, column_offset, spectrum.transpose(2, 0, 1, 3).reshape(2 * slots * blk, columns))
     strips = pl.pallas_call(
         gradient_kernel,
         out_shape=strips_shape,
-        in_specs=[VMEM, ANY] + [VMEM] * 5,
+        in_specs=[VMEM] + [ANY] * 6,
         out_specs=ANY,
         scratch_shapes=[
+            pltpu.VMEM(pupil_modes.shape, bf16),
+            pltpu.VMEM(amplitude.shape, f32),
+            pltpu.VMEM(left.shape, bf16),
+            pltpu.VMEM(right.shape, bf16),
+            pltpu.VMEM(perm.shape, bf16),
             pltpu.VMEM(strips_shape.shape, bf16),
             pltpu.VMEM(strips_shape.shape, bf16),
             pltpu.VMEM((w, rows), bf16),
@@ -290,8 +313,11 @@
             pltpu.SemaphoreType.DMA((led_count,)),
             pltpu.SemaphoreType.DMA((led_count,)),
             pltpu.SemaphoreType.DMA,
+            pltpu.SemaphoreType.DMA((5,)),
         ],
-        compiler_params=limit(collective_id=0, has_side_effects=True),
+        compiler_params=pltpu.CompilerParams(
+            collective_id=0, has_side_effects=True, vmem_limit_bytes=60 * 1024 * 1024
+        ),
         name="window_gradient",
     )(
         line, strips, pupil_modes, amplitude,
@@ -301,8 +327,12 @@
         add_kernel,
         out_shape=jax.ShapeDtypeStruct((slots, blk, 2, columns), f32),
         in_specs=[SMEM, VMEM],
-        out_specs=VMEM,
-        scratch_shapes=[pltpu.VMEM((slots, 2, blk, columns), f32)],
+        out_specs=ANY,
+        scratch_shapes=[
+            pltpu.VMEM((2 * depth, columns), f32),
+            pltpu.VMEM((slots, blk, 2, columns), f32),
+            pltpu.SemaphoreType.DMA((slots,)),
+        ],
         compiler_params=limit(),
         name="add_strips",
     )(column_offset, strips)

time: 71.8 us -> 64.7 us (0.901)
  Pallas kernels: 66.4 us -> 61.3 us
  local copies, waits for them, and re-layouts: 5.17 us -> 3.14 us
    pallas_call x2, Pallas kernels: 62.2 us -> 57.7 us  [the longest x1 56.3 us: shards(): pl.pallas_call(gradient_kernel, out_shape=strips_shape, in_specs=[VMEM] +...]
    unnamed x17 -> x10, local copies, waits for them, and re-layouts: 5.17 us -> 1.48 us
    transpose x0 -> x1, local copies, waits for them, and re-layouts: none -> 1.65 us  [shards(): spectrum.transpose(2, 0, 1, 3).reshape(2 * slots * blk, columns)]
where the time goes in v4:
time: 64.7 us; the launch traced here: 64.5 us
  Pallas kernels  61.3 us (95%)
  local copies, waits for them, and re-layouts  3.14 us (5%)
    pallas_call x1, Pallas kernels, shards(): pl.pallas_call(gradient_kernel, out_shape=strips_shape, in_specs=[VMEM] +...  56.3 us
    pallas_call x1, Pallas kernels, shards(): pl.pallas_call(add_kernel, out_shape=jax.ShapeDtypeStruct((slots, blk, 2,...  3.61 us
    transpose x1, local copies, waits for them, and re-layouts, shards(): spectrum.transpose(2, 0, 1, 3).reshape(2 * slots * blk, columns)  1.65 us
    unnamed x10, local copies, waits for them, and re-layouts  1.48 us
    pallas_call x1, Pallas kernels, shards(): pl.pallas_call(functools.partial(crop_kernel, slots), out_shape=(strips_s...  1.37 us

profile of v4, /device:TPU:1, one launch (start us, length us, event | category | flops | bytes accessed | tf_op | source)
XLA Modules:
  0.0 64.5 jit_solution(6504955352920673322)
XLA Ops:
  0.0 0.0 copy-start.2
  0.0 0.0 copy-start.4
  0.0 0.0 copy-start.3
  0.0 1.7 %copy.10 = bf16[2,3,16,6144]{3,2,1,0:T(8,128)(2,1)S(1)} copy(bf16[2,3,16,6144]{3,0,2,1:T(2,128)(2,1)} %bitcast.3) | data formatting | bytes 2359296 | tf_op jit(solution)/shard_map/transpose | solution.py:291
  1.7 0.0 copy-done.2
  1.7 0.0 copy-done.4
  1.7 0.0 copy-done.3
  1.7 1.4 %crop_windows.1 = (bf16[16,48,512]{2,1,0:T(8,128)(2,1)S(1)}, s32[8,768]{1,0:T(8,128)S(1)}) custom-call(s32[24]{0:T(128)S(1)} %copy-done.3, s32[16]{0:T(128)S(1)} %copy-done.4, s32[16]{0:T(128)S(1)} %copy-done.2, bf16[96,6144]{1,0:T(8,128)(2,1)S(1)} %bitcast.2), custom_call_target="tpu_custom_call" | custom-call | tf_op jit(solution)/shard_map/crop_windows/pallas_call | solution.py:283
  3.1 0.0 copy-start
  3.1 0.9 %copy-done = bf16[16,48,512]{2,1,0:T(8,128)(2,1)} copy-done((bf16[16,48,512]{2,1,0:T(8,128)(2,1)}, bf16[16,48,512]{2,1,0:T(8,128)(2,1)S(1)}, u32[]{:S(2)}) %copy-start) | copy-done | bytes 786456
  4.0 0.0 copy-start.1
  4.0 0.6 copy-done.1
  4.6 56.3 %window_gradient.1.strips_ref = bf16[16,48,512]{2,1,0:T(8,128)(2,1)} custom-call(s32[8,768]{1,0:T(8,128)} %copy-done.1, bf16[16,48,512]{2,1,0:T(8,128)(2,1)} %copy-done, bf16[8,2,256,256]{3,2,1,0:T(8,128)(2,1)} %pupil_hbm.1, f32[1,512,512]{2,1,0:T(8,128)} %amp_hbm.1, bf16[2,512,256]{2,1,0:T(8,128)(2,1)} %constant.6.clone.left_hbm, ...), custom_call_target="tpu_custom_call" | custom-call | tf_op jit(solution)/shard_map/window_gradient/pallas_call | solution.py:292
  60.8 3.6 %add_strips.1 = f32[3,16,2,6144]{3,2,1,0:T(2,128)} custom-call(s32[16]{0:T(128)} %column_ref.3, bf16[16,48,512]{2,1,0:T(8,128)(2,1)} %window_gradient.1.strips_ref), custom_call_target="tpu_custom_call" | custom-call | tf_op jit(solution)/shard_map/add_strips/pallas_call | solution.py:326
Async XLA Ops:
  0.0 1.7 %copy-start.2 = (s32[16]{0:T(128)S(1)}, s32[16]{0:T(128)}, u32[]{:S(2)}) copy-start(s32[16]{0:T(128)} %column_ref.3) | copy-start | bytes 196
  0.0 1.7 %copy-start.4 = (s32[16]{0:T(128)S(1)}, s32[16]{0:T(128)}, u32[]{:S(2)}) copy-start(s32[16]{0:T(128)} %row_ref.1) | copy-start | bytes 196
  0.0 1.7 %copy-start.3 = (s32[24]{0:T(128)S(1)}, s32[24]{0:T(128)}, u32[]{:S(2)}) copy-start(s32[24]{0:T(128)} %owner_ref.1) | copy-start | bytes 292
  3.1 0.9 %copy-start = (bf16[16,48,512]{2,1,0:T(8,128)(2,1)}, bf16[16,48,512]{2,1,0:T(8,128)(2,1)S(1)}, u32[]{:S(2)}) copy-start(bf16[16,48,512]{2,1,0:T(8,128)(2,1)S(1)} %get-tuple-element.8.strips) | copy-start | bytes 2359300
  4.0 0.6 copy-start.1
